TPU v7x, 32 devices: a whole 2x2x4 slice. The times are simulated.
32 devices in a mesh: dp: 4 (over y, core), space: 8 (over z, x).
Axes of the slice: x: 2, y: 2, z: 4, core: 2. Of those that a mesh axis runs over, the one named last changes fastest.
Arguments:
- features: bfloat16 [4, 8, 48, 512], P('dp', 'space'), may hold values from -6 to 6
- device_block: int32 [4, 8], P('dp'), may hold values from 0 to 15, as said below
- conv_first: bfloat16 [48, 27, 48], replicated, may hold values from -0.15625 to 0.15625
- conv_second: bfloat16 [48, 27, 48], replicated, may hold values from -0.15625 to 0.15625
- head_weight: bfloat16 [3, 48], replicated, may hold values from -0.875 to 0.875
- targets: int32 [4, 8, 3, 512], P('dp', 'space'), may hold values 0 or 1
Outputs:
- affinity_logits: float32 [4, 8, 3, 512], P('dp', 'space')
- grad_first: float32 [48, 27, 48], replicated
- grad_second: float32 [48, 27, 48], replicated
- grad_head: float32 [3, 48], replicated
Inputs may be any that keep to these rules, and one draw needn't show every extreme that they name: `device_block`: row n lists 8 distinct block ids of crop n, one for each device; id = (4 * bx + by) + bz. Blocks that no device lists hold no tissue.
All inputs are finite; a program needn't handle non-finite values. No bound on the sum of `targets` on one device may be relied on, other than what follows from the above.
Results may differ from a plain program's by a relative error of at most 0.0041.
Values may be sent and summed in bfloat16 or wider, within the bound.
No kernel may reach another device: no remote copies, remote signals or barrier semaphores. Data moves between devices by JAX's collectives and lax.ppermute only.
A program may use at most 64 MiB of HBM per device.

v0:
```python
import functools

import jax
import jax.numpy as jnp
from jax import lax
from jax.experimental import pallas as pl
from jax.experimental.pallas import tpu as pltpu
from jax.sharding import PartitionSpec as P

BS = 8


tap_offsets = [
    (tap_index // 9 - 1, tap_index // 3 % 3 - 1, tap_index % 3 - 1) for tap_index in range(27)
]


def elu_pair(values):
    negative = jnp.exp(jnp.minimum(values, 0.0))
    return (jnp.where(values > 0, values, negative - 1.0), jnp.where(values > 0, 1.0, negative))


def neighbor_tables(device_block):
    space_count = lax.axis_size("space")
    depth_z = space_count // 8
    self_index = lax.axis_index("space")
    blocks = device_block[0]
    coords = jnp.stack([blocks // (4 * depth_z), blocks // depth_z % 4, blocks % depth_z])
    own_coords = lax.dynamic_index_in_dim(coords, self_index, 1, keepdims=False)
    offsets = jnp.array(tap_offsets, jnp.int32)
    limits = jnp.array([4, 4, depth_z], jnp.int32)
    wanted = own_coords[None, :] + offsets
    inside = jnp.all((wanted >= 0) & (wanted < limits[None, :]), axis=1) & (jnp.arange(27) != 13)
    wanted_id = (wanted[:, 0] * 4 + wanted[:, 1]) * depth_z + wanted[:, 2]
    matches = (blocks[None, :] == wanted_id[:, None]) & inside[:, None]
    devices = jnp.arange(space_count, dtype=jnp.int32)
    owner_row = jnp.sum(jnp.where(matches, devices[None, :], 0), axis=1)
    present = jnp.any(matches, axis=1)
    relative = coords - own_coords[:, None]
    adjacent = jnp.all(jnp.abs(relative) <= 1, axis=0) & (devices != self_index)
    send_tap = jnp.where(
        adjacent, (relative[0] + 1) * 9 + (relative[1] + 1) * 3 + relative[2] + 1, 13
    )
    return (owner_row, present, send_tap)


def region_slice(block_data, offset, depth_cells):
    span_list = []
    for step_value in offset:
        if step_value == 1:
            span_list.append(slice(BS - depth_cells, BS))
        elif step_value == -1:
            span_list.append(slice(0, depth_cells))
        else:
            span_list.append(slice(0, BS))
    return block_data[:, span_list[0], span_list[1], span_list[2]]


def surround(block_data, depth_cells, tables):
    owner_row, present, send_tap = tables
    channels = block_data.shape[0]
    length = depth_cells * BS * BS
    pieces = []
    for tap_index in range(27):
        if tap_index == 13:
            pieces.append(jnp.zeros((channels, length), block_data.dtype))
        else:
            region = region_slice(block_data, tap_offsets[tap_index], depth_cells).reshape(
                channels, -1
            )
            pieces.append(jnp.pad(region, ((0, 0), (0, length - region.shape[1]))))
    outgoing = jnp.stack(pieces)
    sending = outgoing[send_tap]
    by_source = lax.all_to_all(sending, "space", split_axis=0, concat_axis=0, tiled=True)
    incoming = jnp.where(
        present[:, None, None], by_source[owner_row], jnp.zeros((), block_data.dtype)
    )
    rows_x = []
    for step_x in range(3):
        rows_y = []
        for step_y in range(3):
            rows_z = []
            for step_z in range(3):
                tap_index = step_x * 9 + step_y * 3 + step_z
                if tap_index == 13:
                    rows_z.append(block_data)
                else:
                    extent_list = [
                        BS if step_value == 1 else depth_cells
                        for step_value in (step_x, step_y, step_z)
                    ]
                    count_cells = extent_list[0] * extent_list[1] * extent_list[2]
                    rows_z.append(
                        incoming[tap_index][:, :count_cells].reshape(
                            channels, extent_list[0], extent_list[1], extent_list[2]
                        )
                    )
            rows_y.append(jnp.concatenate(rows_z, axis=3))
        rows_x.append(jnp.concatenate(rows_y, axis=2))
    return jnp.concatenate(rows_x, axis=1)


def conv_padded(padded, kernel, dilation):
    result = lax.conv_general_dilated(
        padded[None],
        kernel,
        (1, 1, 1),
        "VALID",
        rhs_dilation=(dilation, dilation, dilation),
        dimension_numbers=("NCDHW", "OIDHW", "NCDHW"),
        preferred_element_type=jnp.float32,
    )
    return result[0].reshape(kernel.shape[0], BS * BS * BS)


def kernel_grad(padded, grad_rows, dilation):
    channels = padded.shape[0]
    outputs = grad_rows.shape[0]
    grad_block = grad_rows.reshape(outputs, 1, BS, BS, BS)
    result = lax.conv_general_dilated(
        padded[None],
        grad_block,
        (dilation, dilation, dilation),
        "VALID",
        dimension_numbers=("CNDHW", "OIDHW", "NCDHW"),
        preferred_element_type=jnp.float32,
    )
    return result.reshape(channels, outputs, 27).transpose(1, 2, 0)


def on_device_deep(features, device_block, conv_first, conv_second, head_weight, targets):
    channels = features.shape[2]
    tables = neighbor_tables(device_block)
    kernel_first = conv_first.reshape(channels, 3, 3, 3, channels).transpose(0, 4, 1, 2, 3)
    kernel_second = conv_second.reshape(channels, 3, 3, 3, channels).transpose(0, 4, 1, 2, 3)
    block_in = features[0, 0].reshape(channels, BS, BS, BS)
    padded_in = surround(block_in, 1, tables)
    pre_first = conv_padded(padded_in, kernel_first, 1)
    act_first, slope_first = elu_pair(pre_first)
    hid_first = act_first.astype(jnp.bfloat16)
    padded_first = surround(hid_first.reshape(channels, BS, BS, BS), 2, tables)
    pre_second = conv_padded(padded_first, kernel_second, 2)
    act_second, slope_second = elu_pair(pre_second)
    hid_second = act_second.astype(jnp.bfloat16)
    logits = jnp.dot(head_weight, hid_second, preferred_element_type=jnp.float32)
    scale = (lax.axis_size("dp") * lax.axis_size("space") * 3 * BS * BS * BS) ** (-0.5)
    grad_logit = ((jax.nn.sigmoid(logits) - targets[0, 0].astype(jnp.float32)) * scale).astype(
        jnp.bfloat16
    )
    grad_head = lax.dot_general(
        grad_logit, hid_second, (((1,), (1,)), ((), ())), preferred_element_type=jnp.float32
    )
    back_second = lax.dot_general(
        head_weight, grad_logit, (((0,), (0,)), ((), ())), preferred_element_type=jnp.float32
    )
    grad_pre_second = (back_second * slope_second).astype(jnp.bfloat16)
    grad_second = kernel_grad(padded_first, grad_pre_second, 2)
    padded_grad = surround(grad_pre_second.reshape(channels, BS, BS, BS), 2, tables)
    kernel_back = jnp.transpose(kernel_second[:, :, ::-1, ::-1, ::-1], (1, 0, 2, 3, 4))
    back_first = conv_padded(padded_grad, kernel_back, 2)
    grad_pre_first = (back_first * slope_first).astype(jnp.bfloat16)
    grad_first = kernel_grad(padded_in, grad_pre_first, 1)
    grad_first, grad_second, grad_head = lax.psum(
        (grad_first, grad_second, grad_head), ("dp", "space")
    )
    return (logits[None, None], grad_first, grad_second, grad_head)


C = 48
CELLS = 512
ROWS = 1008
LANES = 128


def lanes(rows=1):
    return lax.broadcasted_iota(jnp.int32, (rows, LANES), 1)


def pack_kernel(features_ref, targets_ref, out_ref):
    targets = targets_ref[:, 0, :].astype(jnp.float32)
    targets = jnp.concatenate([targets, jnp.zeros((1, CELLS), jnp.float32)], axis=0)
    pieces = [targets[:, LANES * q : LANES * (q + 1)] for q in range(4)]
    target_tile = jnp.concatenate(pieces, axis=0).astype(jnp.bfloat16)
    for ct in range(3):
        for q in range(4):
            out_ref[4 * ct + q] = features_ref[
                16 * ct : 16 * (ct + 1), LANES * q : LANES * (q + 1)
            ]
    out_ref[12] = target_tile


def weights_kernel(first_ref, second_ref, head_ref, w1_ref, w2_ref, w2t_ref, h_ref, ht_ref):
    for ref, out in ((first_ref, w1_ref), (second_ref, w2_ref)):
        stacked = []
        for a in range(3):
            taps = [ref[9 * a + t].astype(jnp.float32) for t in range(9)]
            stacked.append(jnp.concatenate(taps, axis=1))
        whole = jnp.concatenate(stacked, axis=0)
        out[...] = whole.astype(jnp.bfloat16)
        if out is w2_ref:
            w2t_ref[...] = whole.T.astype(jnp.bfloat16)
    head = jnp.concatenate(
        [head_ref[...].astype(jnp.float32), jnp.zeros((13, C), jnp.float32)], axis=0
    )
    h_ref[...] = head.astype(jnp.bfloat16)
    ht_ref[...] = head.T.astype(jnp.bfloat16)


def matmul(left, right):
    return lax.dot_general(
        left, right, (((1,), (0,)), ((), ())), preferred_element_type=jnp.float32
    )


def matmul_lanes(left, right):
    return lax.dot_general(
        left, right, (((1,), (1,)), ((), ())), preferred_element_type=jnp.float32
    )


def roll(values, shift):
    return pltpu.roll(values, shift % LANES, 1)


def crop_kernel(
    scale,
    block_ref,
    gathered_ref,
    w1_hbm,
    w2_hbm,
    w2t_hbm,
    h_hbm,
    ht_hbm,
    logits_ref,
    packed_ref,
    table_ref,
    present_ref,
    x9_ref,
    h9_ref,
    product_ref,
    slope1_ref,
    slope2_ref,
    hid2_ref,
    grad2_ref,
    shifted_ref,
    back_ref,
    w1_ref,
    w2_ref,
    w2t_ref,
    h_ref,
    ht_ref,
    sems,
):
    sources = (w1_hbm, w2_hbm, w2t_hbm, h_hbm, ht_hbm)
    copies = [
        pltpu.make_async_copy(source, target, sems.at[k])
        for k, (source, target) in enumerate(zip(sources, (w1_ref, w2_ref, w2t_ref, h_ref, ht_ref)))
    ]
    for copy in copies:
        copy.start()

    count = gathered_ref.shape[0]
    me = lax.axis_index("space")
    own = block_ref[0, me]
    for slot in range(10):
        table_ref[slot] = 0
        present_ref[slot] = 0
    for s in range(count):
        block = block_ref[0, s]
        dx = (block >> 2) - (own >> 2) + 1
        dy = (block & 3) - (own & 3) + 1
        near = (dx >= 0) & (dx <= 2) & (dy >= 0) & (dy <= 2)
        slot = jnp.where(near, dx * 3 + dy, 9)
        table_ref[slot] = s
        present_ref[slot] = 1
    owner = [table_ref[q] for q in range(9)]
    there = [present_ref[q].astype(jnp.float32) for q in range(9)]

    lane = lanes()
    depth = lane & 7
    low, mid = lane < 32, lane < 96
    own_lanes = ((lane >= 32) & (lane < 96)).astype(jnp.float32)
    left_half = lane < 64
    masks = [
        jnp.where(low, there[3 * bx], jnp.where(mid, there[3 * bx + 1], there[3 * bx + 2]))
        for bx in range(3)
    ]
    edge_masks = [jnp.where(left_half, there[3 * bx + 2], there[3 * bx]) for bx in range(3)]

    for plane in range(18):
        bx, i = (plane + 3) // 8, (plane + 3) % 8
        q, half = i // 2, i % 2
        for ct in range(3):
            parts = [
                gathered_ref[owner[3 * bx + by], 4 * ct + q].astype(jnp.float32) for by in range(3)
            ]
            before = roll(parts[0], 96 - 64 * half)
            middle = roll(parts[1], 32 - 64 * half)
            after = roll(parts[2], 96 - 64 * half)
            main = jnp.where(low, before, jnp.where(mid, middle, after)) * masks[bx]
            edge = jnp.where(left_half, after, before) * edge_masks[bx]
            for c in (-1, 0, 1):
                if c == 0:
                    main_c, edge_c = main, edge
                else:
                    keep = depth >= 1 if c == 1 else depth <= 6
                    main_c, edge_c = jnp.where(keep, main, 0.0), jnp.where(keep, edge, 0.0)
                for b in (-1, 0, 1):
                    step = 8 * b + c
                    if b == 1:
                        source = jnp.where(lane < step, edge_c, main_c)
                    elif b == -1:
                        source = jnp.where(lane >= LANES + step, edge_c, main_c)
                    else:
                        source = main_c
                    row = (3 * (b + 1) + c + 1) * C + 16 * ct
                    x9_ref[row : row + 16, LANES * plane : LANES * (plane + 1)] = (
                        roll(source, -step) if step else source
                    ).astype(jnp.bfloat16)

    def plane_cols(plane):
        return slice(LANES * plane, LANES * (plane + 1))

    def summed(plane, stride):
        return (
            product_ref[0:C, plane_cols(plane)]
            + product_ref[C : 2 * C, plane_cols(plane + stride)]
            + product_ref[2 * C : 3 * C, plane_cols(plane + 2 * stride)]
        )

    for copy in copies:
        copy.wait()
    for n in range(9):
        cols = slice(256 * n, 256 * (n + 1))
        product_ref[:, cols] = matmul(w1_ref[...], x9_ref[:, cols])

    for plane in range(16):
        bx = (plane + 4) // 8
        pre = summed(plane, 1)
        negative = jnp.exp(jnp.minimum(pre, 0.0))
        if 4 <= plane < 12:
            slope1_ref[:, plane_cols(plane - 4)] = jnp.where(pre > 0, 1.0, negative)
        hidden = jnp.where(pre > 0, pre, negative - 1.0) * masks[bx]
        hidden = hidden.astype(jnp.bfloat16).astype(jnp.float32)
        for c in (-1, 0, 1):
            if c == 0:
                source = hidden
            else:
                source = jnp.where(depth >= 2 if c == 1 else depth <= 5, hidden, 0.0)
            for b in (-1, 0, 1):
                step = 16 * b + 2 * c
                row = (3 * (b + 1) + c + 1) * C
                h9_ref[row : row + C, plane_cols(plane)] = (
                    roll(source, -step) if step else source
                ).astype(jnp.bfloat16)

    for n in range(8):
        cols = slice(256 * n, 256 * (n + 1))
        product_ref[:, cols] = matmul(w2_ref[...], h9_ref[:, cols])

    for plane in range(12):
        bx = (plane + 6) // 8
        pre = summed(plane, 2)
        negative = jnp.exp(jnp.minimum(pre, 0.0))
        slope2_ref[:, plane_cols(plane)] = jnp.where(pre > 0, 1.0, negative) * masks[bx]
        hidden = jnp.where(pre > 0, pre, negative - 1.0) * masks[bx]
        hid2_ref[:, plane_cols(plane)] = hidden.astype(jnp.bfloat16)

    logits = matmul(h_ref[...], hid2_ref[...])
    targets = []
    for half in range(2):
        row = []
        for bx in range(3):
            parts = [gathered_ref[owner[3 * bx + by], 12].astype(jnp.float32) for by in range(3)]
            before = roll(parts[0], 96 - 64 * half)
            middle = roll(parts[1], 32 - 64 * half)
            after = roll(parts[2], 96 - 64 * half)
            row.append(jnp.where(low, before, jnp.where(mid, middle, after)))
        targets.append(row)
    grads = []
    for plane in range(12):
        bx, i = (plane + 6) // 8, (plane + 6) % 8
        value = logits[:, plane_cols(plane)]
        wanted = targets[i % 2][bx][4 * (i // 2) : 4 * (i // 2) + 4]
        wanted = jnp.concatenate([wanted, jnp.zeros((12, LANES), jnp.float32)], axis=0)
        sigmoid = 1.0 / (1.0 + jnp.exp(-value))
        grads.append((sigmoid - wanted) * masks[bx] * scale)
    for q in range(4):
        first = roll(logits[:, plane_cols(2 + 2 * q)], -32)
        second = roll(logits[:, plane_cols(3 + 2 * q)], 32)
        logits_ref[:, 0, plane_cols(q)] = jnp.where(left_half, first, second)[0:3]

    grad_logit = jnp.concatenate(grads, axis=1).astype(jnp.bfloat16)
    back = matmul(ht_ref[...], grad_logit)
    grad2_ref[...] = (back * slope2_ref[...]).astype(jnp.bfloat16)
    own_grads = jnp.concatenate([grads[2 + x] * own_lanes for x in range(8)], axis=1)
    head_part = matmul_lanes(hid2_ref[:, 2 * LANES : 10 * LANES], own_grads.astype(jnp.bfloat16))

    own_bf16 = own_lanes.astype(jnp.bfloat16)
    shifted_ref[...] = jnp.zeros_like(shifted_ref)
    for a in range(3):
        for x in range(8):
            shifted_ref[C * a : C * (a + 1), plane_cols(x + 2 * a)] = (
                grad2_ref[:, plane_cols(x + 2)] * own_bf16
            )
    second_part = matmul_lanes(shifted_ref[...], h9_ref[:, 2 * LANES : 14 * LANES])

    for a in range(3):
        for x in range(8):
            shifted_ref[C * a : C * (a + 1), plane_cols(x)] = grad2_ref[:, plane_cols(x + 4 - 2 * a)]
    for n in range(4):
        cols = slice(256 * n, 256 * (n + 1))
        back_ref[:, cols] = matmul(w2t_ref[...], shifted_ref[:, cols])
    grad1 = []
    for x in range(8):
        total = jnp.zeros((C, LANES), jnp.float32)
        for c in (-1, 0, 1):
            part = jnp.zeros((C, LANES), jnp.float32)
            for b in (-1, 0, 1):
                row = (3 * (b + 1) + c + 1) * C
                step = 16 * b + 2 * c
                piece = back_ref[row : row + C, plane_cols(x)]
                part += roll(piece, step) if step else piece
            if c:
                part = jnp.where(depth >= 2 if c == 1 else depth <= 5, part, 0.0)
            total += part
        grad1.append((total * slope1_ref[:, plane_cols(x)] * own_lanes).astype(jnp.bfloat16))

    shifted_ref[...] = jnp.zeros_like(shifted_ref)
    for a in range(3):
        for x in range(8):
            shifted_ref[C * a : C * (a + 1), plane_cols(x + a)] = grad1[x]
    first_part = matmul_lanes(
        shifted_ref[:, 0 : 10 * LANES], x9_ref[:, 4 * LANES : 14 * LANES]
    )

    for q in range(3):
        cols = plane_cols(q)
        packed_ref[144 * q : 144 * (q + 1), :] = first_part[:, cols].astype(jnp.bfloat16)
        packed_ref[144 * (q + 3) : 144 * (q + 4), :] = second_part[:, cols].astype(jnp.bfloat16)
    head_part = jnp.concatenate([head_part, jnp.zeros((96, 16), jnp.float32)], axis=0)
    tail = jnp.concatenate(
        [first_part[:, 384:], second_part[:, 384:], head_part, jnp.zeros((144, 16), jnp.float32)],
        axis=1,
    )
    packed_ref[144 * 6 : ROWS, :] = tail.astype(jnp.bfloat16)
    packed_ref[ROWS:, :] = jnp.zeros((packed_ref.shape[0] - ROWS, LANES), jnp.bfloat16)


def sum_kernel(parts_ref, out_ref):
    total = parts_ref[0].astype(jnp.float32)
    for s in range(1, parts_ref.shape[0]):
        total += parts_ref[s].astype(jnp.float32)
    out_ref[...] = total.astype(jnp.bfloat16)


def unpack_kernel(rows_ref, first_ref, second_ref, head_ref):
    tail = rows_ref[144 * 6 : ROWS, :].astype(jnp.float32)
    for k, out in ((0, first_ref), (1, second_ref)):
        tiles = [rows_ref[144 * (3 * k + q) : 144 * (3 * k + q + 1), :].astype(jnp.float32) for q in range(3)]
        whole = jnp.concatenate(tiles + [tail[:, C * k : C * (k + 1)]], axis=1)
        for a in range(3):
            for t in range(9):
                out[9 * a + t] = whole[C * a : C * (a + 1), C * t : C * (t + 1)]
    head_ref[...] = tail[0:C, 96:112].T[0:3]


def on_device_flat(features, device_block, conv_first, conv_second, head_weight, targets):
    space_count = lax.axis_size("space")
    device_count = lax.axis_size("dp") * space_count
    bf16, f32 = jnp.bfloat16, jnp.float32
    shape = jax.ShapeDtypeStruct
    vmem = pl.BlockSpec(memory_space=pltpu.VMEM)
    smem = pl.BlockSpec(memory_space=pltpu.SMEM)

    packed_block = pl.pallas_call(
        pack_kernel,
        out_shape=shape((13, 16, LANES), bf16),
        in_specs=[vmem] * 2,
        out_specs=vmem,
        name="pack_block",
    )(features[0, 0], targets[0].transpose(1, 0, 2))
    gathered = lax.all_gather(packed_block, "space")
    w1, w2, w2t, head, head_t = pl.pallas_call(
        weights_kernel,
        out_shape=(
            shape((3 * C, 9 * C), bf16),
            shape((3 * C, 9 * C), bf16),
            shape((9 * C, 3 * C), bf16),
            shape((16, C), bf16),
            shape((C, 16), bf16),
        ),
        in_specs=[vmem] * 3,
        out_specs=(vmem,) * 5,
        name="lay_out_weights",
    )(conv_first.transpose(1, 0, 2), conv_second.transpose(1, 0, 2), head_weight)

    chunk = -(-ROWS // (16 * device_count)) * 16
    scale = (device_count * 3 * CELLS) ** (-0.5)
    logits, packed = pl.pallas_call(
        functools.partial(crop_kernel, scale),
        out_shape=(shape((3, 1, CELLS), f32), shape((chunk * device_count, LANES), bf16)),
        in_specs=[smem, vmem] + [pl.BlockSpec(memory_space=pltpu.HBM)] * 5,
        out_specs=(vmem, vmem),
        scratch_shapes=[
            pltpu.SMEM((10,), jnp.int32),
            pltpu.SMEM((10,), jnp.int32),
            pltpu.VMEM((9 * C, 18 * LANES), bf16),
            pltpu.VMEM((9 * C, 16 * LANES), bf16),
            pltpu.VMEM((3 * C, 18 * LANES), f32),
            pltpu.VMEM((C, 8 * LANES), f32),
            pltpu.VMEM((C, 12 * LANES), f32),
            pltpu.VMEM((C, 12 * LANES), bf16),
            pltpu.VMEM((C, 12 * LANES), bf16),
            pltpu.VMEM((3 * C, 12 * LANES), bf16),
            pltpu.VMEM((9 * C, 8 * LANES), f32),
            pltpu.VMEM((3 * C, 9 * C), bf16),
            pltpu.VMEM((3 * C, 9 * C), bf16),
            pltpu.VMEM((9 * C, 3 * C), bf16),
            pltpu.VMEM((16, C), bf16),
            pltpu.VMEM((C, 16), bf16),
            pltpu.SemaphoreType.DMA((5,)),
        ],
        compiler_params=pltpu.CompilerParams(vmem_limit_bytes=40 * 1024 * 1024),
        name="forward_backward",
    )(device_block, gathered, w1, w2, w2t, head, head_t)

    terms = lax.all_to_all(
        packed.reshape(device_count, chunk, LANES), ("dp", "space"), 0, 0, tiled=True
    )
    summed = pl.pallas_call(
        sum_kernel,
        out_shape=shape((chunk, LANES), bf16),
        in_specs=[vmem],
        out_specs=vmem,
        compiler_params=pltpu.CompilerParams(vmem_limit_bytes=16 * 1024 * 1024),
        name="sum_terms",
    )(terms)
    rows = lax.all_gather(summed, ("dp", "space"))
    grad_first, grad_second, grad_head = pl.pallas_call(
        unpack_kernel,
        out_shape=(shape((27, C, C), f32), shape((27, C, C), f32), shape((3, C), f32)),
        in_specs=[vmem],
        out_specs=(vmem,) * 3,
        compiler_params=pltpu.CompilerParams(vmem_limit_bytes=16 * 1024 * 1024),
        name="unpack_gradients",
    )(rows.reshape(device_count * chunk, LANES))
    return (
        logits.transpose(1, 0, 2)[None],
        grad_first.transpose(1, 0, 2),
        grad_second.transpose(1, 0, 2),
        grad_head,
    )


def solution(mesh):
    in_specs = (
        P("dp", "space", None, None),
        P("dp", None),
        P(),
        P(),
        P(),
        P("dp", "space", None, None),
    )
    out_specs = (P("dp", "space", None, None), P(), P(), P())
    depth_z = mesh.shape["space"] // 8
    return jax.shard_map(
        on_device_flat if depth_z == 1 else on_device_deep,
        mesh=mesh,
        in_specs=in_specs,
        out_specs=out_specs,
        check_vma=False,
    )
```

profile of v0, /device:TPU:0, one launch (start us, length us, event | category | flops | bytes accessed | tf_op | source)
XLA Modules:
  0.0 133.2 jit_solution(13738191835450595721)
XLA Ops:
  0.6 1.4 %pack_block.1 = bf16[13,16,128]{2,1,0:T(8,128)(2,1)} custom-call(bf16[48,512]{1,0:T(8,128)(2,1)} %bitcast.15, s32[3,1,512]{2,1,0:T(1,128)} %bitcast.16), custom_call_target="tpu_custom_call" | custom-call | tf_op jit(solution)/shard_map/pack_block/pallas_call | solution.py:476
  2.1 33.0 %all-gather = bf16[104,16,128]{2,1,0:T(8,128)(2,1)S(1)} all-gather(bf16[13,16,128]{2,1,0:T(8,128)(2,1)} %pack_block.1), channel_id=2, replica_groups=mesh['dp'=4,'space'=8] {'space'}, dimensions={0}, use_global_device_ids=true | all-gather | bytes 479232 | tf_op jit(solution)/shard_map/all_gather | solution.py:483
  35.1 2.1 %lay_out_weights.1 = (bf16[144,432]{1,0:T(8,128)(2,1)}, bf16[144,432]{1,0:T(8,128)(2,1)}, bf16[432,144]{1,0:T(8,128)(2,1)}, bf16[16,48]{1,0:T(8,128)(2,1)}, bf16[48,16]{1,0:T(8,128)(2,1)}) custom-call(bf16[27,48,48]{2,1,0:T(8,128)(2,1)} %bitcast.13, bf16[27,48,48]{2,1,0:T(8,128)(2,1)} %bitcast.14, bf16[3,48]{1,0:T(4,128)(2,1)} %head_ref.1), custom_call_target="tpu_custom_call" | custom-call | tf_op jit(solution)/shard_map/lay_out_weights/pallas_call | solution.py:484
  37.2 0.0 copy-start.4
  37.2 0.0 copy-start.5
  37.2 0.7 copy-done.4
  37.9 0.0 copy-done.5
  37.9 0.0 copy-start
  37.9 0.9 copy-done
  38.8 0.0 copy-start.1
  38.8 0.9 copy-done.1
  39.7 0.0 copy-start.2
  39.7 0.9 copy-done.2
  40.6 0.0 copy-start.3
  40.6 0.7 copy-done.3
  41.3 8.3 %forward_backward.1 = (f32[3,1,512]{2,1,0:T(1,128)}, bf16[1024,128]{1,0:T(8,128)(2,1)S(1)}) custom-call(s32[1,8]{1,0:T(1,128)S(1)} %copy-done.5, bf16[8,13,16,128]{3,2,1,0:T(8,128)(2,1)S(1)} %bitcast.11, bf16[144,432]{1,0:T(8,128)(2,1)S(1)} %copy-done.1, bf16[144,432]{1,0:T(8,128)(2,1)S(1)} %copy-done.2, bf16[432,144]{1,0:T(8,128)(2,1)S(1)} %copy-done, ...), custom_call_target="tpu_custom_call" | custom-call | tf_op jit(solution)/shard_map/forward_backward/pallas_call | solution.py:500
  49.7 16.1 %all_to_all.5.parts_ref = bf16[32,32,128]{2,1,0:T(8,128)(2,1)S(1)} all-to-all(bf16[32,32,128]{2,1,0:T(8,128)(2,1)S(1)} %bitcast.12), channel_id=1, replica_groups=mesh['dp'=4,'space'=8] {'dp','space'}, dimensions={0} | all-to-all | bytes 524288 | tf_op jit(solution)/shard_map/all_to_all | solution.py:528
  65.9 66.1 %all-gather.1.rows_ref = bf16[1024,128]{1,0:T(8,128)(2,1)S(1)} all-gather(bf16[32,128]{1,0:T(8,128)(2,1)S(1)} %sum_terms.1), channel_id=3, replica_groups=mesh['dp'=4,'space'=8] {'dp','space'}, dimensions={0}, use_global_device_ids=true | all-gather | bytes 270336 | tf_op jit(solution)/shard_map/all_gather | solution.py:539
  132.0 1.2 unpack_gradients.1
  (1 shorter events, 0.0 us)
Async XLA Ops:
  37.2 0.7 copy-start.4
  37.2 0.7 copy-start.5
  37.9 0.9 copy-start
  38.8 0.9 copy-start.1
  39.7 0.9 copy-start.2
  40.6 0.7 copy-start.3
where the time goes:
time: 134 us; the launch traced here: 133 us
  blocking collectives  115 us (86%)
  Pallas kernels  13.2 us (10%)
  local copies, waits for them, and re-layouts  4.15 us (3%)
    all_gather x1, blocking collectives, on_device_flat(): rows = lax.all_gather(summed, ('dp', 'space'))  66.1 us
    all_gather x1, blocking collectives, on_device_flat(): gathered = lax.all_gather(packed_block, 'space')  33 us
    all_to_all x1, blocking collectives, on_device_flat(): lax.all_to_all(packed.reshape(device_count, chunk, LANES), ('dp', 'space'...  16.1 us
    pallas_call x1, Pallas kernels, on_device_flat(): pl.pallas_call(functools.partial(crop_kernel, scale), out_shape=(shape((3...  8.35 us
    unnamed x12, local copies, waits for them, and re-layouts  4.15 us

commit v1 on v0

--- a/solution.py
+++ b/solution.py
@@ -189,21 +189,12 @@
     out_ref[12] = target_tile
 
 
-def weights_kernel(first_ref, second_ref, head_ref, w1_ref, w2_ref, w2t_ref, h_ref, ht_ref):
-    for ref, out in ((first_ref, w1_ref), (second_ref, w2_ref)):
-        stacked = []
-        for a in range(3):
-            taps = [ref[9 * a + t].astype(jnp.float32) for t in range(9)]
-            stacked.append(jnp.concatenate(taps, axis=1))
-        whole = jnp.concatenate(stacked, axis=0)
-        out[...] = whole.astype(jnp.bfloat16)
-        if out is w2_ref:
-            w2t_ref[...] = whole.T.astype(jnp.bfloat16)
-    head = jnp.concatenate(
-        [head_ref[...].astype(jnp.float32), jnp.zeros((13, C), jnp.float32)], axis=0
-    )
-    h_ref[...] = head.astype(jnp.bfloat16)
-    ht_ref[...] = head.T.astype(jnp.bfloat16)
+def stacked_taps(ref):
+    rows = []
+    for a in range(3):
+        taps = [ref[9 * a + t].astype(jnp.float32) for t in range(9)]
+        rows.append(jnp.concatenate(taps, axis=1))
+    return jnp.concatenate(rows, axis=0)
 
 
 def matmul(left, right):
@@ -224,13 +215,20 @@
 
 def crop_kernel(
     scale,
+    count,
+    *refs,
+):
+    blocks, refs = refs[1 : 1 + count], refs[:1] + refs[1 + count :]
+    crop_body(scale, blocks, *refs)
+
+
+def crop_body(
+    scale,
+    blocks,
     block_ref,
-    gathered_ref,
-    w1_hbm,
-    w2_hbm,
-    w2t_hbm,
-    h_hbm,
-    ht_hbm,
+    first_ref,
+    second_ref,
+    head_ref,
     logits_ref,
     packed_ref,
     table_ref,
@@ -244,22 +242,23 @@
     grad2_ref,
     shifted_ref,
     back_ref,
+    gathered_ref,
     w1_ref,
     w2_ref,
     w2t_ref,
-    h_ref,
-    ht_ref,
-    sems,
 ):
-    sources = (w1_hbm, w2_hbm, w2t_hbm, h_hbm, ht_hbm)
-    copies = [
-        pltpu.make_async_copy(source, target, sems.at[k])
-        for k, (source, target) in enumerate(zip(sources, (w1_ref, w2_ref, w2t_ref, h_ref, ht_ref)))
-    ]
-    for copy in copies:
-        copy.start()
-
-    count = gathered_ref.shape[0]
+    count = len(blocks)
+    for k in range(count):
+        gathered_ref[k] = blocks[k][...]
+    w1_ref[...] = stacked_taps(first_ref).astype(jnp.bfloat16)
+    whole = stacked_taps(second_ref)
+    w2_ref[...] = whole.astype(jnp.bfloat16)
+    w2t_ref[...] = whole.T.astype(jnp.bfloat16)
+    head = head_ref[...].astype(jnp.float32)
+    head = jnp.concatenate([head, jnp.zeros((13, C), jnp.float32)], axis=0)
+    head_t = head.T.astype(jnp.bfloat16)
+    head = head.astype(jnp.bfloat16)
+
     me = lax.axis_index("space")
     own = block_ref[0, me]
     for slot in range(10):
@@ -271,7 +270,7 @@
         dy = (block & 3) - (own & 3) + 1
         near = (dx >= 0) & (dx <= 2) & (dy >= 0) & (dy <= 2)
         slot = jnp.where(near, dx * 3 + dy, 9)
-        table_ref[slot] = s
+        table_ref[slot] = s ^ me
         present_ref[slot] = 1
     owner = [table_ref[q] for q in range(9)]
     there = [present_ref[q].astype(jnp.float32) for q in range(9)]
@@ -328,8 +327,6 @@
             + product_ref[2 * C : 3 * C, plane_cols(plane + 2 * stride)]
         )
 
-    for copy in copies:
-        copy.wait()
     for n in range(9):
         cols = slice(256 * n, 256 * (n + 1))
         product_ref[:, cols] = matmul(w1_ref[...], x9_ref[:, cols])
@@ -366,7 +363,7 @@
         hidden = jnp.where(pre > 0, pre, negative - 1.0) * masks[bx]
         hid2_ref[:, plane_cols(plane)] = hidden.astype(jnp.bfloat16)
 
-    logits = matmul(h_ref[...], hid2_ref[...])
+    logits = matmul(head, hid2_ref[...])
     targets = []
     for half in range(2):
         row = []
@@ -391,7 +388,7 @@
         logits_ref[:, 0, plane_cols(q)] = jnp.where(left_half, first, second)[0:3]
 
     grad_logit = jnp.concatenate(grads, axis=1).astype(jnp.bfloat16)
-    back = matmul(ht_ref[...], grad_logit)
+    back = matmul(head_t, grad_logit)
     grad2_ref[...] = (back * slope2_ref[...]).astype(jnp.bfloat16)
     own_grads = jnp.concatenate([grads[2 + x] * own_lanes for x in range(8)], axis=1)
     head_part = matmul_lanes(hid2_ref[:, 2 * LANES : 10 * LANES], own_grads.astype(jnp.bfloat16))
@@ -451,7 +448,9 @@
     total = parts_ref[0].astype(jnp.float32)
     for s in range(1, parts_ref.shape[0]):
         total += parts_ref[s].astype(jnp.float32)
-    out_ref[...] = total.astype(jnp.bfloat16)
+    total = total.astype(jnp.bfloat16)
+    for s in range(out_ref.shape[0]):
+        out_ref[s] = total
 
 
 def unpack_kernel(rows_ref, first_ref, second_ref, head_ref):
@@ -469,6 +468,7 @@
     space_count = lax.axis_size("space")
     device_count = lax.axis_size("dp") * space_count
     bf16, f32 = jnp.bfloat16, jnp.float32
+    small = pltpu.CompilerParams(vmem_limit_bytes=8 * 1024 * 1024)
     shape = jax.ShapeDtypeStruct
     vmem = pl.BlockSpec(memory_space=pltpu.VMEM)
     smem = pl.BlockSpec(memory_space=pltpu.SMEM)
@@ -478,29 +478,20 @@
         out_shape=shape((13, 16, LANES), bf16),
         in_specs=[vmem] * 2,
         out_specs=vmem,
+        compiler_params=small,
         name="pack_block",
     )(features[0, 0], targets[0].transpose(1, 0, 2))
-    gathered = lax.all_gather(packed_block, "space")
-    w1, w2, w2t, head, head_t = pl.pallas_call(
-        weights_kernel,
-        out_shape=(
-            shape((3 * C, 9 * C), bf16),
-            shape((3 * C, 9 * C), bf16),
-            shape((9 * C, 3 * C), bf16),
-            shape((16, C), bf16),
-            shape((C, 16), bf16),
-        ),
-        in_specs=[vmem] * 3,
-        out_specs=(vmem,) * 5,
-        name="lay_out_weights",
-    )(conv_first.transpose(1, 0, 2), conv_second.transpose(1, 0, 2), head_weight)
+    blocks = [packed_block] + [
+        lax.ppermute(packed_block, "space", [(s, s ^ k) for s in range(space_count)])
+        for k in range(1, space_count)
+    ]
 
     chunk = -(-ROWS // (16 * device_count)) * 16
     scale = (device_count * 3 * CELLS) ** (-0.5)
     logits, packed = pl.pallas_call(
-        functools.partial(crop_kernel, scale),
+        functools.partial(crop_kernel, scale, space_count),
         out_shape=(shape((3, 1, CELLS), f32), shape((chunk * device_count, LANES), bf16)),
-        in_specs=[smem, vmem] + [pl.BlockSpec(memory_space=pltpu.HBM)] * 5,
+        in_specs=[smem] + [vmem] * (space_count + 3),
         out_specs=(vmem, vmem),
         scratch_shapes=[
             pltpu.SMEM((10,), jnp.int32),
@@ -514,35 +505,39 @@
             pltpu.VMEM((C, 12 * LANES), bf16),
             pltpu.VMEM((3 * C, 12 * LANES), bf16),
             pltpu.VMEM((9 * C, 8 * LANES), f32),
+            pltpu.VMEM((space_count, 13, 16, LANES), bf16),
             pltpu.VMEM((3 * C, 9 * C), bf16),
             pltpu.VMEM((3 * C, 9 * C), bf16),
             pltpu.VMEM((9 * C, 3 * C), bf16),
-            pltpu.VMEM((16, C), bf16),
-            pltpu.VMEM((C, 16), bf16),
-            pltpu.SemaphoreType.DMA((5,)),
         ],
-        compiler_params=pltpu.CompilerParams(vmem_limit_bytes=40 * 1024 * 1024),
+        compiler_params=pltpu.CompilerParams(vmem_limit_bytes=20 * 1024 * 1024),
         name="forward_backward",
-    )(device_block, gathered, w1, w2, w2t, head, head_t)
+    )(
+        device_block,
+        *blocks,
+        conv_first.transpose(1, 0, 2),
+        conv_second.transpose(1, 0, 2),
+        head_weight,
+    )
 
     terms = lax.all_to_all(
         packed.reshape(device_count, chunk, LANES), ("dp", "space"), 0, 0, tiled=True
     )
     summed = pl.pallas_call(
         sum_kernel,
-        out_shape=shape((chunk, LANES), bf16),
+        out_shape=shape((device_count, chunk, LANES), bf16),
         in_specs=[vmem],
         out_specs=vmem,
-        compiler_params=pltpu.CompilerParams(vmem_limit_bytes=16 * 1024 * 1024),
+        compiler_params=small,
         name="sum_terms",
     )(terms)
-    rows = lax.all_gather(summed, ("dp", "space"))
+    rows = lax.all_to_all(summed, ("dp", "space"), 0, 0, tiled=True)
     grad_first, grad_second, grad_head = pl.pallas_call(
         unpack_kernel,
         out_shape=(shape((27, C, C), f32), shape((27, C, C), f32), shape((3, C), f32)),
         in_specs=[vmem],
         out_specs=(vmem,) * 3,
-        compiler_params=pltpu.CompilerParams(vmem_limit_bytes=16 * 1024 * 1024),
+        compiler_params=small,
         name="unpack_gradients",
     )(rows.reshape(device_count * chunk, LANES))
     return (

time: 134 us -> 56.1 us (0.42)
  blocking collectives: 115 us -> 28.4 us
  starting transfers between devices: 0 us -> 12.5 us
  Pallas kernels: 13.2 us -> 6.41 us
  waiting for transfers between devices: 0 us -> 3.71 us
    all_gather x2 -> x0, blocking collectives: 99.1 us -> none  [the longest x1 66.1 us: on_device_flat(): rows = lax.all_gather(summed, ('dp', 'space'))]
    all_to_all x0 -> x1, blocking collectives: none -> 12.8 us  [on_device_flat(): rows = lax.all_to_all(summed, ('dp', 'space'), 0, 0, tiled=True)]
    ppermute x0 -> x7, starting transfers between devices: none -> 12.5 us  [on_device_flat(): lax.ppermute(packed_block, 'space', [(s, s ^ k) for s in range(space_coun...]
    pallas_call x3 -> x2, Pallas kernels: 10.5 us -> 5.15 us  [the longest x1 5.1 us: on_device_flat(): pl.pallas_call(functools.partial(crop_kernel, scale, space_count), out_sh...]
    ppermute x0 -> x7, waiting for transfers between devices: none -> 3.71 us  [on_device_flat(): lax.ppermute(packed_block, 'space', [(s, s ^ k) for s in range(space_coun...]
    pallas_call x1, Pallas kernels: 1.44 us -> 0.02 us  [on_device_flat(): pl.pallas_call(pack_kernel, out_shape=shape((13, 16, LANES), bf16), in_sp...]
  transfers between devices with their start and end apart: 0 -> 7, of which waited for: 0 -> 5; matrix products, arithmetic and copies ran while one was open for 0% -> 0% of each run, Pallas kernels for 0% -> 0%
where the time goes in v1:
time: 56.1 us; the launch traced here: 55.8 us
  blocking collectives  28.4 us (51%)
  starting transfers between devices  12.5 us (22%)
  Pallas kernels  6.41 us (11%)
  local copies, waits for them, and re-layouts  4.11 us (7%)
  waiting for transfers between devices  3.71 us (7%)
  between operations  0.66 us (1%)
    all_to_all x1, blocking collectives, on_device_flat(): lax.all_to_all(packed.reshape(device_count, chunk, LANES), ('dp', 'space'...  15.6 us
    all_to_all x1, blocking collectives, on_device_flat(): rows = lax.all_to_all(summed, ('dp', 'space'), 0, 0, tiled=True)  12.8 us
    ppermute x7, starting transfers between devices, on_device_flat(): lax.ppermute(packed_block, 'space', [(s, s ^ k) for s in range(space_coun...  12.5 us
    pallas_call x1, Pallas kernels, on_device_flat(): pl.pallas_call(functools.partial(crop_kernel, scale, space_count), out_sh...  5.1 us
    unnamed x12, local copies, waits for them, and re-layouts  4.11 us
    ppermute x7, waiting for transfers between devices, on_device_flat(): lax.ppermute(packed_block, 'space', [(s, s ^ k) for s in range(space_coun...  3.71 us
    pallas_call x1, Pallas kernels, on_device_flat(): pl.pallas_call(unpack_kernel, out_shape=(shape((27, C, C), f32), shape((2...  1.24 us
  transfers between devices with their start and end apart: 7, of which 5 were waited for; matrix products, arithmetic and copies ran while one was open for 0% of the time, Pallas kernels for 0%

profile of v1, /device:TPU:0, one launch (start us, length us, event | category | flops | bytes accessed | tf_op | source)
XLA Modules:
  0.0 55.8 jit_solution(2493516863281661210)
XLA Ops:
  0.6 0.0 copy-start.2
  0.6 0.8 %copy-done.2 = bf16[1,1,48,512]{3,2,1,0:T(8,128)(2,1)S(1)} copy-done((bf16[1,1,48,512]{3,2,1,0:T(8,128)(2,1)S(1)}, bf16[1,1,48,512]{3,2,1,0:T(8,128)(2,1)}, u32[]{:S(2)}) %copy-start.2) | copy-done | bytes 49176
  1.4 0.0 copy-start.3
  1.4 0.7 %copy-done.3 = s32[1,1,3,512]{3,1,2,0:T(1,128)S(1)} copy-done((s32[1,1,3,512]{3,1,2,0:T(1,128)S(1)}, s32[1,1,3,512]{3,1,2,0:T(1,128)}, u32[]{:S(2)}) %copy-start.3) | copy-done | bytes 6168
  2.1 6.0 %collective-permute-start.6 = (bf16[13,16,128]{2,1,0:T(8,128)(2,1)S(1)}, bf16[13,16,128]{2,1,0:T(8,128)(2,1)S(1)}, u32[]{:S(2)}, u32[]{:S(2)}) collective-permute-start(bf16[13,16,128]{2,1,0:T(8,128)(2,1)S(1)} %pack_block.1.refs_1_), channel_id=1, source_target_pairs={{0,7},{1,6},{2,5},{3,4},{4,3},{5,2},{6,1},{7,0},{8,15},{9,14},{10,... | collective-permute-start | bytes 159752 | tf_op jit(solution)/shard_map/ppermute | solution.py:485
  8.2 0.2 collective-permute-start.5
  8.4 0.8 %collective-permute-start.4 = (bf16[13,16,128]{2,1,0:T(8,128)(2,1)S(1)}, bf16[13,16,128]{2,1,0:T(8,128)(2,1)S(1)}, u32[]{:S(2)}, u32[]{:S(2)}) collective-permute-start(bf16[13,16,128]{2,1,0:T(8,128)(2,1)S(1)} %pack_block.1.refs_1_), channel_id=1, source_target_pairs={{0,5},{1,4},{2,7},{3,6},{4,1},{5,0},{6,3},{7,2},{8,13},{9,12},{10,... | collective-permute-start | bytes 159752 | tf_op jit(solution)/shard_map/ppermute | solution.py:485
  9.2 2.0 %collective-permute-start.3 = (bf16[13,16,128]{2,1,0:T(8,128)(2,1)S(1)}, bf16[13,16,128]{2,1,0:T(8,128)(2,1)S(1)}, u32[]{:S(2)}, u32[]{:S(2)}) collective-permute-start(bf16[13,16,128]{2,1,0:T(8,128)(2,1)S(1)} %pack_block.1.refs_1_), channel_id=1, source_target_pairs={{0,4},{1,5},{2,6},{3,7},{4,0},{5,1},{6,2},{7,3},{8,12},{9,13},{10,... | collective-permute-start | bytes 159752 | tf_op jit(solution)/shard_map/ppermute | solution.py:485
  11.2 2.3 %collective-permute-start.2 = (bf16[13,16,128]{2,1,0:T(8,128)(2,1)S(1)}, bf16[13,16,128]{2,1,0:T(8,128)(2,1)S(1)}, u32[]{:S(2)}, u32[]{:S(2)}) collective-permute-start(bf16[13,16,128]{2,1,0:T(8,128)(2,1)S(1)} %pack_block.1.refs_1_), channel_id=1, source_target_pairs={{0,3},{1,2},{2,1},{3,0},{4,7},{5,6},{6,5},{7,4},{8,11},{9,10},{10,... | collective-permute-start | bytes 159752 | tf_op jit(solution)/shard_map/ppermute | solution.py:485
  13.5 0.0 collective-permute-done.6.refs_8_
  13.5 0.8 %collective-permute-start.1 = (bf16[13,16,128]{2,1,0:T(8,128)(2,1)S(1)}, bf16[13,16,128]{2,1,0:T(8,128)(2,1)S(1)}, u32[]{:S(2)}, u32[]{:S(2)}) collective-permute-start(bf16[13,16,128]{2,1,0:T(8,128)(2,1)S(1)} %pack_block.1.refs_1_), channel_id=1, source_target_pairs={{0,2},{1,3},{2,0},{3,1},{4,6},{5,7},{6,4},{7,5},{8,10},{9,11},{10,... | collective-permute-start | bytes 159752 | tf_op jit(solution)/shard_map/ppermute | solution.py:485
  14.3 0.0 collective-permute-done.5.refs_7_
  14.3 0.4 collective-permute-start
  14.7 1.8 %collective-permute-done.4.refs_6_ = bf16[13,16,128]{2,1,0:T(8,128)(2,1)S(1)} collective-permute-done((bf16[13,16,128]{2,1,0:T(8,128)(2,1)S(1)}, bf16[13,16,128]{2,1,0:T(8,128)(2,1)S(1)}, u32[]{:S(2)}, u32[]{:S(2)}) %collective-permute-start.4) | collective-permute-done | bytes 53280 | tf_op jit(solution)/shard_map/ppermute | solution.py:485
  16.5 0.9 %collective-permute-done.3.refs_5_ = bf16[13,16,128]{2,1,0:T(8,128)(2,1)S(1)} collective-permute-done((bf16[13,16,128]{2,1,0:T(8,128)(2,1)S(1)}, bf16[13,16,128]{2,1,0:T(8,128)(2,1)S(1)}, u32[]{:S(2)}, u32[]{:S(2)}) %collective-permute-start.3) | collective-permute-done | bytes 53280 | tf_op jit(solution)/shard_map/ppermute | solution.py:485
  17.4 0.4 collective-permute-done.2.refs_4_
  17.8 0.2 collective-permute-done.1.refs_3_
  18.0 0.4 collective-permute-done.refs_2_
  18.4 0.0 copy-start.4
  18.4 0.0 copy-start.5
  18.4 0.7 %copy-done.4 = bf16[3,48]{1,0:T(4,128)(2,1)S(1)} copy-done((bf16[3,48]{1,0:T(4,128)(2,1)S(1)}, bf16[3,48]{1,0:T(4,128)(2,1)}, u32[]{:S(2)}) %copy-start.4) | copy-done | bytes 312
  19.1 0.0 copy-done.5
  19.1 0.0 copy-start
  19.1 1.0 %copy-done = bf16[48,27,48]{2,0,1:T(8,128)(2,1)S(1)} copy-done((bf16[48,27,48]{2,0,1:T(8,128)(2,1)S(1)}, bf16[48,27,48]{2,0,1:T(8,128)(2,1)}, u32[]{:S(2)}) %copy-start) | copy-done | bytes 124440
  20.1 0.0 copy-start.1
  20.1 1.0 %copy-done.1 = bf16[48,27,48]{2,0,1:T(8,128)(2,1)S(1)} copy-done((bf16[48,27,48]{2,0,1:T(8,128)(2,1)S(1)}, bf16[48,27,48]{2,0,1:T(8,128)(2,1)}, u32[]{:S(2)}) %copy-start.1) | copy-done | bytes 124440
  21.0 5.1 %forward_backward.1 = (f32[3,1,512]{2,1,0:T(1,128)}, bf16[1024,128]{1,0:T(8,128)(2,1)S(1)}) custom-call(s32[1,8]{1,0:T(1,128)S(1)} %copy-done.5, bf16[13,16,128]{2,1,0:T(8,128)(2,1)S(1)} %pack_block.1.refs_1_, bf16[13,16,128]{2,1,0:T(8,128)(2,1)S(1)} %collective-permute-done.refs_2_, bf16[13,16,128]{2,1,0:T(8,128)(2,1)S(1)} %collective-permute-done.1.refs_3_, ...), custom_call_target="tpu_custom_call" | custom-call | tf_op jit(solution)/shard_map/forward_backward/pallas_call | solution.py:491
  26.1 15.6 %all_to_all.10.parts_ref = bf16[32,32,128]{2,1,0:T(8,128)(2,1)S(1)} all-to-all(bf16[32,32,128]{2,1,0:T(8,128)(2,1)S(1)} %bitcast.14), channel_id=1, replica_groups=mesh['dp'=4,'space'=8] {'dp','space'}, dimensions={0} | all-to-all | bytes 524288 | tf_op jit(solution)/shard_map/all_to_all | solution.py:523
  41.7 0.1 sum_terms.1
  41.8 12.8 %all_to_all.11 = bf16[32,32,128]{2,1,0:T(8,128)(2,1)S(1)} all-to-all(bf16[32,32,128]{2,1,0:T(8,128)(2,1)S(1)} %sum_terms.1), channel_id=1, replica_groups=mesh['dp'=4,'space'=8] {'dp','space'}, dimensions={0} | all-to-all | bytes 524288 | tf_op jit(solution)/shard_map/all_to_all | solution.py:534
  54.6 1.2 %unpack_gradients.1 = (f32[27,48,48]{2,1,0:T(8,128)}, f32[27,48,48]{2,1,0:T(8,128)}, f32[3,48]{1,0:T(4,128)}) custom-call(bf16[1024,128]{1,0:T(8,128)(2,1)S(1)} %bitcast.11), custom_call_target="tpu_custom_call" | custom-call | tf_op jit(solution)/shard_map/unpack_gradients/pallas_call | solution.py:535
  (1 shorter events, 0.0 us)
Async XLA Ops:
  0.6 0.8 %copy-start.2 = (bf16[1,1,48,512]{3,2,1,0:T(8,128)(2,1)S(1)}, bf16[1,1,48,512]{3,2,1,0:T(8,128)(2,1)}, u32[]{:S(2)}) copy-start(bf16[1,1,48,512]{3,2,1,0:T(8,128)(2,1)} %param.6) | copy-start | bytes 147460
  1.4 0.7 %copy-start.3 = (s32[1,1,3,512]{3,1,2,0:T(1,128)S(1)}, s32[1,1,3,512]{3,1,2,0:T(1,128)}, u32[]{:S(2)}) copy-start(s32[1,1,3,512]{3,1,2,0:T(1,128)} %param.11) | copy-start | bytes 18436
  2.1 11.3 %collective-permute-start.6 = (bf16[13,16,128]{2,1,0:T(8,128)(2,1)S(1)}, bf16[13,16,128]{2,1,0:T(8,128)(2,1)S(1)}, u32[]{:S(2)}, u32[]{:S(2)}) collective-permute-start(bf16[13,16,128]{2,1,0:T(8,128)(2,1)S(1)} %pack_block.1.refs_1_), channel_id=1, source_target_pairs={{0,7},{1,6},{2,5},{3,4},{4,3},{5,2},{6,1},{7,0},{8,15},{9,14},{10,... | collective-permute-start | bytes 159752 | tf_op jit(solution)/shard_map/ppermute | solution.py:485
  8.2 6.1 %collective-permute-start.5 = (bf16[13,16,128]{2,1,0:T(8,128)(2,1)S(1)}, bf16[13,16,128]{2,1,0:T(8,128)(2,1)S(1)}, u32[]{:S(2)}, u32[]{:S(2)}) collective-permute-start(bf16[13,16,128]{2,1,0:T(8,128)(2,1)S(1)} %pack_block.1.refs_1_), channel_id=1, source_target_pairs={{0,6},{1,7},{2,4},{3,5},{4,2},{5,3},{6,0},{7,1},{8,14},{9,15},{10,... | collective-permute-start | bytes 159752 | tf_op jit(solution)/shard_map/ppermute | solution.py:485
  8.4 8.1 %collective-permute-start.4 = (bf16[13,16,128]{2,1,0:T(8,128)(2,1)S(1)}, bf16[13,16,128]{2,1,0:T(8,128)(2,1)S(1)}, u32[]{:S(2)}, u32[]{:S(2)}) collective-permute-start(bf16[13,16,128]{2,1,0:T(8,128)(2,1)S(1)} %pack_block.1.refs_1_), channel_id=1, source_target_pairs={{0,5},{1,4},{2,7},{3,6},{4,1},{5,0},{6,3},{7,2},{8,13},{9,12},{10,... | collective-permute-start | bytes 159752 | tf_op jit(solution)/shard_map/ppermute | solution.py:485
  9.2 8.2 %collective-permute-start.3 = (bf16[13,16,128]{2,1,0:T(8,128)(2,1)S(1)}, bf16[13,16,128]{2,1,0:T(8,128)(2,1)S(1)}, u32[]{:S(2)}, u32[]{:S(2)}) collective-permute-start(bf16[13,16,128]{2,1,0:T(8,128)(2,1)S(1)} %pack_block.1.refs_1_), channel_id=1, source_target_pairs={{0,4},{1,5},{2,6},{3,7},{4,0},{5,1},{6,2},{7,3},{8,12},{9,13},{10,... | collective-permute-start | bytes 159752 | tf_op jit(solution)/shard_map/ppermute | solution.py:485
  11.2 6.6 %collective-permute-start.2 = (bf16[13,16,128]{2,1,0:T(8,128)(2,1)S(1)}, bf16[13,16,128]{2,1,0:T(8,128)(2,1)S(1)}, u32[]{:S(2)}, u32[]{:S(2)}) collective-permute-start(bf16[13,16,128]{2,1,0:T(8,128)(2,1)S(1)} %pack_block.1.refs_1_), channel_id=1, source_target_pairs={{0,3},{1,2},{2,1},{3,0},{4,7},{5,6},{6,5},{7,4},{8,11},{9,10},{10,... | collective-permute-start | bytes 159752 | tf_op jit(solution)/shard_map/ppermute | solution.py:485
  13.5 4.6 %collective-permute-start.1 = (bf16[13,16,128]{2,1,0:T(8,128)(2,1)S(1)}, bf16[13,16,128]{2,1,0:T(8,128)(2,1)S(1)}, u32[]{:S(2)}, u32[]{:S(2)}) collective-permute-start(bf16[13,16,128]{2,1,0:T(8,128)(2,1)S(1)} %pack_block.1.refs_1_), channel_id=1, source_target_pairs={{0,2},{1,3},{2,0},{3,1},{4,6},{5,7},{6,4},{7,5},{8,10},{9,11},{10,... | collective-permute-start | bytes 159752 | tf_op jit(solution)/shard_map/ppermute | solution.py:485
  14.3 4.1 %collective-permute-start = (bf16[13,16,128]{2,1,0:T(8,128)(2,1)S(1)}, bf16[13,16,128]{2,1,0:T(8,128)(2,1)S(1)}, u32[]{:S(2)}, u32[]{:S(2)}) collective-permute-start(bf16[13,16,128]{2,1,0:T(8,128)(2,1)S(1)} %pack_block.1.refs_1_), channel_id=1, source_target_pairs={{0,1},{1,0},{2,3},{3,2},{4,5},{5,4},{6,7},{7,6},{8,9},{9,8},{10,11... | collective-permute-start | bytes 159752 | tf_op jit(solution)/shard_map/ppermute | solution.py:485
  18.4 0.7 %copy-start.4 = (bf16[3,48]{1,0:T(4,128)(2,1)S(1)}, bf16[3,48]{1,0:T(4,128)(2,1)}, u32[]{:S(2)}) copy-start(bf16[3,48]{1,0:T(4,128)(2,1)} %refs_11_.1) | copy-start | bytes 868
  18.4 0.7 %copy-start.5 = (s32[1,8]{1,0:T(1,128)S(1)}, s32[1,8]{1,0:T(1,128)}, u32[]{:S(2)}) copy-start(s32[1,8]{1,0:T(1,128)} %refs_0_.1) | copy-start | bytes 100
  19.1 1.0 %copy-start = (bf16[48,27,48]{2,0,1:T(8,128)(2,1)S(1)}, bf16[48,27,48]{2,0,1:T(8,128)(2,1)}, u32[]{:S(2)}) copy-start(bf16[48,27,48]{2,0,1:T(8,128)(2,1)} %param.8) | copy-start | bytes 373252
  20.1 1.0 %copy-start.1 = (bf16[48,27,48]{2,0,1:T(8,128)(2,1)S(1)}, bf16[48,27,48]{2,0,1:T(8,128)(2,1)}, u32[]{:S(2)}) copy-start(bf16[48,27,48]{2,0,1:T(8,128)(2,1)} %param.9) | copy-start | bytes 373252
